TPU v7x, 128 devices: a whole 4x4x4 slice. The times are simulated.
128 devices in a mesh: row: 8 (over x, z_lo), col: 16 (over y, z_hi, core).
Axes of the slice: x: 4, y: 4, z: 4 (z_hi: 2, z_lo: 2; z = z_hi * 2 + z_lo), core: 2. Of those that a mesh axis runs over, the one named last changes fastest.
Arguments:
- features: bfloat16 [49152, 128], P(('col', 'row'))
- weight: bfloat16 [128, 128], replicated, may hold values from -0.5 to 0.5
- tiles: bfloat16 [8, 16, 864, 128, 128], P('row', 'col'), as said below
- tile_rows: int32 [8, 16, 864], P('row', 'col'), may hold values from 0 to 47, as said below
- tile_cols: int32 [8, 16, 864], P('row', 'col'), may hold values from 0 to 23
- tile_count: int32 [8, 16], P('row', 'col'), may hold values from 216 to 864, as said below
Outputs:
- aggregated: bfloat16 [49152, 128], P(('row', 'col'))
Inputs may be any that keep to these rules, and one draw needn't show every extreme that they name: `tile_rows`: the slots of one block name distinct tiles of its 48 x 24 grid, padded slots included. `tile_count`: some block is full. `tiles`: nonnegative edge weights.
All inputs are finite; a program needn't handle non-finite values.
Results may differ from a plain program's by a relative error of at most 0.019.
Values may be sent and summed in bfloat16 or wider, within the bound.
A program may use at most 256 MiB of HBM per device.

v0:
```python
import jax
import jax.numpy as jnp
from jax import lax
from jax.experimental import pallas as pl
from jax.experimental.pallas import tpu as pltpu
from jax.sharding import PartitionSpec as P

F32, BF16, I32 = jnp.float32, jnp.bfloat16, jnp.int32
SIDE = 128
CHUNK = 32
EXTRA = 16
HALF = 192
ORDER = ((2, 1), (1, 1), (3, 1), (2, 0), (0, 1), (1, 0), (3, 0), (0, 0))


def table(step, values):
    coef = list(values)
    for bit in (1, 2, 4):
        for i in range(8):
            if i & bit:
                coef[i] -= coef[i - bit]
    bits = (step % 2, (step // 2) % 2, step // 4)
    total = coef[0]
    for i in range(1, 8):
        if coef[i]:
            term = coef[i]
            for j in range(3):
                if i >> j & 1:
                    term = term * bits[j]
            total = total + term
    return total


def split_sums(value):
    high = value.astype(BF16)
    low = (value - high.astype(F32)).astype(BF16)
    return jnp.concatenate([high, low], axis=0)


def join_sums(value):
    return value[:8] + value[8:]


def kernel(
    n_row, n_col, slots, row_tiles, col_tiles,
    feat_hbm, weight_hbm, tiles_hbm, rows_hbm, cols_hbm, count_ref, out_hbm,
    tiles, csum, feats, weight, projected, scaled, rows_v, cols_v, slot_v, slot_s, colx,
    full, sib, from_two_lo, from_two_hi, from_lo, from_hi, from_z, out_v,
    tile_sem, local_sem, feat_send, feat_recv, colx_send, colx_recv, sib_send, sib_recv,
    y_send, y_recv, z_send, z_recv,
):
    group = feat_hbm.shape[0]
    owner_tiles = group // SIDE
    step_tiles = 2 * owner_tiles
    row = lax.axis_index("row")
    col = lax.axis_index("col")
    core = col % 2
    z_hi = (col // 2) % 2
    y = col // 4
    sibling = (row, col + 1 - 2 * core)
    y_next = (row, ((y + 1) % 4) * 4 + col % 4)
    y_prev = (row, ((y + 3) % 4) * 4 + col % 4)
    z_other = (row, y * 4 + (1 - z_hi) * 2 + core)
    row_peers = [((row + i) % n_row, col) for i in range(1, n_row)]

    def tile_copy(k):
        part = pl.ds(k * CHUNK, CHUNK)
        return pltpu.make_async_copy(tiles_hbm.at[part], tiles.at[part], tile_sem.at[k])

    def send(src, dst, send_sem, recv_sem, device):
        return pltpu.make_async_remote_copy(
            src_ref=src, dst_ref=dst, send_sem=send_sem, recv_sem=recv_sem,
            device_id=device, device_id_type=pl.DeviceIdType.MESH,
        )

    chunks = slots // CHUNK
    local = [
        pltpu.make_async_copy(cols_hbm, cols_v, local_sem.at[0]),
        pltpu.make_async_copy(rows_hbm, rows_v, local_sem.at[1]),
        pltpu.make_async_copy(weight_hbm, weight, local_sem.at[2]),
        pltpu.make_async_copy(feat_hbm, feats.at[row], local_sem.at[3]),
    ]
    for copy in local:
        copy.start()
    for k in range(chunks):
        tile_copy(k).start()

    barrier = pltpu.get_barrier_semaphore()
    partners = row_peers + [sibling, y_next, y_prev, z_other]
    for device in partners:
        pl.semaphore_signal(barrier, inc=1, device_id=device, device_id_type=pl.DeviceIdType.MESH)
    pl.semaphore_wait(barrier, len(partners))

    feat_copies = [
        send(feat_hbm, feats.at[row], feat_send.at[i], feat_recv.at[i], device)
        for i, device in enumerate(row_peers)
    ]
    for copy in feat_copies:
        copy.start()

    tiles[slots] = jnp.zeros((SIDE, SIDE), BF16)
    scaled[:, SIDE:] = jnp.ones((col_tiles * SIDE, SIDE), BF16)
    count = count_ref[0, 0]
    sublane = lax.broadcasted_iota(I32, (8, SIDE), 0)

    def column_sums(k, carry):
        tile_copy(k).wait()
        for g in range(CHUNK // 8):
            first = k * CHUNK + g * 8
            sums = None
            for s in range(8):
                tile = tiles[first + s].astype(F32)
                part = jnp.sum(tile.reshape(SIDE // 8, 8, SIDE), axis=0)
                part = jnp.broadcast_to(jnp.sum(part, axis=0, keepdims=True), (8, SIDE))
                sums = part if s == 0 else jnp.where(sublane == s, part, sums)
            live = first + sublane < count
            csum[pl.ds(pl.multiple_of(first, 8), 8), :] = jnp.where(live, sums, 0.0)
        return carry

    lax.fori_loop(0, chunks // 2, column_sums, 0)

    for copy in local:
        copy.wait()
    lane = lax.broadcasted_iota(I32, (1, slots), 1)
    place = jnp.where(lane < count, rows_v[...] * 32 + cols_v[...], -1)
    padded = jnp.concatenate([place, jnp.full((1, 7 * SIDE - slots), -1, I32)], axis=1)
    stacked = jnp.concatenate(
        [padded[:, g * SIDE:(g + 1) * SIDE] for g in range(7)] + [jnp.full((SIDE - 7, SIDE), -1, I32)], axis=0
    )
    turned = stacked.T
    places = [jnp.broadcast_to(turned[:, g:g + 1], (SIDE, SIDE)) for g in range(7)]
    slot_id = lax.broadcasted_iota(I32, (SIDE, SIDE), 0)
    lane_id = lax.broadcasted_iota(I32, (SIDE, SIDE), 1)
    slot_v[...] = jnp.full(slot_v.shape, slots, I32)
    for b in range(row_tiles * 32 // SIDE):
        best = jnp.full((SIDE, SIDE), slots, I32)
        for g in range(7):
            best = jnp.where(places[g] == lane_id + b * SIDE, slot_id + g * SIDE, best)
        slot_v[b:b + 1, :] = jnp.min(best, axis=0, keepdims=True)
    to_scalar = pltpu.make_async_copy(slot_v, slot_s, local_sem.at[4])
    to_scalar.start()

    for copy in feat_copies:
        copy.wait_recv()
    for j in range(n_row):
        projected[pl.ds(j * group, group), :] = jnp.dot(
            feats[j], weight[...], preferred_element_type=F32
        )
    to_scalar.wait()

    lax.fori_loop(chunks // 2, chunks, column_sums, 0)

    kind = lax.broadcasted_iota(I32, (col_tiles, slots), 0)
    at = lax.broadcasted_iota(I32, (col_tiles, slots), 1)
    pick = jnp.where((kind == cols_v[...]) & (at < count), 1.0, 0.0).astype(BF16)
    rest = csum[...]
    own = jnp.zeros((col_tiles, SIDE), F32)
    for _ in range(3):
        piece = rest.astype(BF16)
        own = own + jnp.dot(pick, piece, preferred_element_type=F32)
        rest = rest - piece.astype(F32)
    colx[row] = own
    colx_copies = [
        send(colx.at[row], colx.at[row], colx_send.at[i], colx_recv.at[i], device)
        for i, device in enumerate(row_peers)
    ]
    for copy in colx_copies:
        copy.start()
    for copy in colx_copies:
        copy.wait_recv()
    degree = colx[0]
    for j in range(1, n_row):
        degree = degree + colx[j]
    factor = lax.rsqrt(1.0 + degree)
    factor = jnp.concatenate([factor, jnp.ones((SIDE - col_tiles, SIDE), F32)], axis=0).T
    for c in range(col_tiles):
        block = projected[c * SIDE:(c + 1) * SIDE, :] * factor[:, c:c + 1]
        scaled[c * SIDE:(c + 1) * SIDE, :SIDE] = block.astype(BF16)

    eye = jnp.where(slot_id == lane_id, 1.0, 0.0)

    def sib_copy(k):
        return send(full.at[k, 1 - core], sib.at[k], sib_send.at[k], sib_recv.at[k], sibling)

    low, high = pl.ds(0, HALF), pl.ds(HALF, group + EXTRA - HALF)

    def two_copies(k, dz):
        return (
            send(full.at[k, core, low], from_two_lo.at[dz], y_send.at[4 * dz], y_recv.at[4 * dz], y_next),
            send(full.at[k, core, high], from_two_hi.at[dz], y_send.at[4 * dz + 1], y_recv.at[4 * dz + 1], y_prev),
        )

    def lo_copy(k, dz):
        return send(full.at[k, core], from_lo.at[dz], y_send.at[4 * dz + 2], y_recv.at[4 * dz + 2], y_next)

    def hi_copy(k, dz):
        return send(full.at[k, core], from_hi.at[dz], y_send.at[4 * dz + 3], y_recv.at[4 * dz + 3], y_prev)

    def z_copy(k):
        return send(full.at[k, core], from_z, z_send, z_recv, z_other)

    def add_up(k, others):
        total = full[k, core].astype(F32) + sib[k].astype(F32)
        for other in others:
            total = total + other[...].astype(F32)
        return total

    def keep(k, total):
        full[k, core, pl.ds(0, group), :] = total[:group].astype(BF16)
        full[k, core, pl.ds(group, EXTRA), :] = split_sums(join_sums(total[group:]))

    index = {pair: k for k, pair in enumerate(ORDER)}

    def pass_on(k):
        dy, dz = ORDER[k]
        sib_copy(k).wait_recv()
        if dy == 2:
            keep(k, add_up(k, []))
            for copy in two_copies(k, dz):
                copy.start()
        elif dy == 1:
            two_copies(index[2, dz], dz)[0].wait_recv()
            total = add_up(k, [])
            top = total[:HALF] + from_two_lo[dz].astype(F32)
            keep(k, jnp.concatenate([top, total[HALF:]], axis=0))
            lo_copy(k, dz).start()
        elif dy == 3:
            two_copies(index[2, dz], dz)[1].wait_recv()
            total = add_up(k, [])
            bottom = total[HALF:] + from_two_hi[dz].astype(F32)
            keep(k, jnp.concatenate([total[:HALF], bottom], axis=0))
            hi_copy(k, dz).start()
        elif dz == 1:
            lo_copy(index[1, 1], 1).wait_recv()
            hi_copy(index[3, 1], 1).wait_recv()
            keep(k, add_up(k, [from_lo.at[1], from_hi.at[1]]))
            z_copy(k).start()

    def product(k, carry):
        chip = ((y + table(k, [d[0] for d in ORDER])) % 4) * 2 + (z_hi + table(k, [d[1] for d in ORDER])) % 2
        first = chip * step_tiles
        wide = []
        for a in range(step_tiles):
            at_row = first + a
            wide.append(jnp.concatenate(
                [tiles[slot_s[at_row // 4, (at_row % 4) * 32 + c]] for c in range(col_tiles)], axis=1
            ))
        result = jnp.dot(jnp.concatenate(wide, axis=0), scaled[...], preferred_element_type=F32)
        for h in range(2):
            part = result[h * group:(h + 1) * group]
            full[k, h, pl.ds(0, group), :] = part[:, :SIDE].astype(BF16)
            sums = [
                jnp.sum(part[i * SIDE:(i + 1) * SIDE, SIDE:] * eye, axis=0, keepdims=True)
                for i in range(owner_tiles)
            ]
            sums.append(jnp.zeros((8 - owner_tiles, SIDE), F32))
            full[k, h, pl.ds(group, EXTRA), :] = split_sums(jnp.concatenate(sums, axis=0))
        sib_copy(k).start()
        for done in range(7):
            @pl.when(k == done + 1)
            def _():
                pass_on(done)
        return carry

    lax.fori_loop(0, 8, product, 0)

    last = index[0, 0]
    sib_copy(last).wait_recv()
    lo_copy(index[1, 0], 0).wait_recv()
    hi_copy(index[3, 0], 0).wait_recv()
    z_copy(index[0, 1]).wait_recv()
    total = add_up(last, [from_lo.at[0], from_hi.at[0], from_z])
    norm = lax.rsqrt(1.0 + join_sums(total[group:]))
    norm = jnp.concatenate([norm, jnp.ones((SIDE - 8, SIDE), F32)], axis=0).T
    for i in range(owner_tiles):
        out_v[i * SIDE:(i + 1) * SIDE, :] = (total[i * SIDE:(i + 1) * SIDE] * norm[:, i:i + 1]).astype(BF16)
    store = pltpu.make_async_copy(out_v, out_hbm, local_sem.at[5])
    store.start()

    for copy in feat_copies + colx_copies:
        copy.wait_send()
    for k, (dy, dz) in enumerate(ORDER):
        sib_copy(k).wait_send()
        if dy == 2:
            for copy in two_copies(k, dz):
                copy.wait_send()
        elif dy == 1:
            lo_copy(k, dz).wait_send()
        elif dy == 3:
            hi_copy(k, dz).wait_send()
        elif dz == 1:
            z_copy(k).wait_send()
    store.wait()


def body(features, weight, tiles, tile_rows, tile_cols, tile_count):
    n_row, n_col = lax.axis_size("row"), lax.axis_size("col")
    group, width = features.shape
    hidden = weight.shape[1]
    slots, side = tiles.shape[2], tiles.shape[3]
    row_tiles = n_col * group // side
    col_tiles = n_row * group // side
    block = group + EXTRA
    dma = pltpu.SemaphoreType.DMA

    def run(*refs):
        kernel(n_row, n_col, slots, row_tiles, col_tiles, *refs)

    anywhere = pl.BlockSpec(memory_space=pl.ANY)
    return pl.pallas_call(
        run,
        out_shape=jax.ShapeDtypeStruct((group, hidden), BF16),
        in_specs=[anywhere] * 5 + [pl.BlockSpec(memory_space=pltpu.SMEM)],
        out_specs=anywhere,
        scratch_shapes=[
            pltpu.VMEM((slots + 1, side, side), BF16),
            pltpu.VMEM((slots, side), F32),
            pltpu.VMEM((n_row, group, width), BF16),
            pltpu.VMEM((width, hidden), BF16),
            pltpu.VMEM((col_tiles * side, hidden), F32),
            pltpu.VMEM((col_tiles * side, 2 * hidden), BF16),
            pltpu.VMEM((1, slots), I32),
            pltpu.VMEM((1, slots), I32),
            pltpu.VMEM((16, side), I32),
            pltpu.SMEM((16, side), I32),
            pltpu.VMEM((n_row, col_tiles, side), F32),
            pltpu.VMEM((8, 2, block, hidden), BF16),
            pltpu.VMEM((8, block, hidden), BF16),
            pltpu.VMEM((2, HALF, hidden), BF16),
            pltpu.VMEM((2, block - HALF, hidden), BF16),
            pltpu.VMEM((2, block, hidden), BF16),
            pltpu.VMEM((2, block, hidden), BF16),
            pltpu.VMEM((block, hidden), BF16),
            pltpu.VMEM((group, hidden), BF16),
            dma((slots // CHUNK,)),
            dma((6,)),
            dma((n_row - 1,)),
            dma((n_row - 1,)),
            dma((n_row - 1,)),
            dma((n_row - 1,)),
            dma((8,)),
            dma((8,)),
            dma((8,)),
            dma((8,)),
            dma,
            dma,
        ],
        compiler_params=pltpu.CompilerParams(
            collective_id=0, has_side_effects=True, vmem_limit_bytes=56 * 2**20
        ),
    )(
        features, weight, tiles.reshape(slots, side, side),
        tile_rows.reshape(1, slots), tile_cols.reshape(1, slots), tile_count.reshape(1, 1),
    )


def solution(mesh):
    in_specs = (
        P(("col", "row"), None),
        P(),
        P("row", "col", None, None, None),
        P("row", "col", None),
        P("row", "col", None),
        P("row", "col"),
    )
    out_specs = P(("row", "col"), None)
    return jax.shard_map(body, mesh=mesh, in_specs=in_specs, out_specs=out_specs, check_vma=False)
```

profile of v0, /device:TPU:0, one launch (start us, length us, event | category | flops | bytes accessed | tf_op | source)
XLA Modules:
  0.0 49.0 jit_solution(13806473076173616727)
XLA Ops:
  0.7 46.8 %shard_map.64 = bf16[384,128]{1,0:T(8,128)(2,1)} custom-call(bf16[384,128]{1,0:T(8,128)(2,1)} %refs_0_.1, bf16[128,128]{1,0:T(8,128)(2,1)} %refs_1_.1, bf16[864,128,128]{2,1,0:T(8,128)(2,1)} %bitcast.3, s32[1,864]{1,0:T(1,128)} %bitcast.4, s32[1,864]{1,0:T(1,128)} %bitcast.5, s32[1,1]{1,0:T(1,128)S(6)} %copy.8.refs_5_), custom_call_target="tpu_custom_call" | custom-call | tf_op jit(solution)/shard_map/pallas_call | solution.py:310
  47.5 1.5 %copy.9 = bf16[384,128]{1,0:T(8,128)(2,1)} copy(bf16[384,128]{1,0:T(8,128)(2,1)} %shard_map.64) | data formatting | bytes 196608
where the time goes:
time: 49.1 us; the launch traced here: 49 us
  Pallas kernels  46.8 us (95%)
  local copies, waits for them, and re-layouts  1.54 us (3%)
  between operations  0.66 us (1%)
    pallas_call x1, Pallas kernels, body(): pl.pallas_call(run, out_shape=jax.ShapeDtypeStruct((group, hidden), BF16)...  46.8 us
    unnamed x1, local copies, waits for them, and re-layouts  1.54 us

commit v1 on v0

v1 whole, which is shorter than its diff:
```python
import jax
import jax.numpy as jnp
from jax import lax
from jax.experimental import pallas as pl
from jax.experimental.pallas import tpu as pltpu
from jax.sharding import PartitionSpec as P

F32, BF16, I32 = jnp.float32, jnp.bfloat16, jnp.int32
SIDE = 128
CHUNK = 32
EXTRA = 16
FIRST = 3
AHEAD = 10
ORDER = ((2, 1), (1, 1), (3, 1), (2, 0), (0, 1), (1, 0), (3, 0), (0, 0))


def table(step, values):
    coef = list(values)
    for bit in (1, 2, 4):
        for i in range(8):
            if i & bit:
                coef[i] -= coef[i - bit]
    bits = (step % 2, (step // 2) % 2, step // 4)
    total = coef[0]
    for i in range(1, 8):
        if coef[i]:
            term = coef[i]
            for j in range(3):
                if i >> j & 1:
                    term = term * bits[j]
            total = total + term
    return total


def split_sums(value):
    high = value.astype(BF16)
    low = (value - high.astype(F32)).astype(BF16)
    return jnp.concatenate([high, low], axis=0)


def join_sums(value):
    return value[:8] + value[8:]


def kernel(
    n_row, n_col, slots, row_tiles, col_tiles,
    feat_hbm, weight_hbm, tiles_hbm, rows_hbm, cols_hbm, count_hbm, out_ref,
    tiles, csum, count_s, feats, weight, projected, scaled, rows_v, cols_v, slot_v, slot_s, colx,
    full, sib, land,
    tile_sem, local_sem, feat_send, feat_recv, colx_send, colx_recv, sib_send, sib_recv,
    own_send, own_recv, y_two, z_one, z_two,
):
    group = feat_hbm.shape[0]
    owner_tiles = group // SIDE
    step_tiles = 2 * owner_tiles
    row = lax.axis_index("row")
    col = lax.axis_index("col")
    core = col % 2
    z_hi = (col // 2) % 2
    y = col // 4
    sibling = (row, col + 1 - 2 * core)

    def chip_peer(dy, dz):
        return (row, (((y + dy) % 4) * 2 + (z_hi + dz) % 2) * 2 + core)

    row_peers = [((row + i) % n_row, col) for i in range(1, n_row)]

    def tile_copy(k):
        part = pl.ds(k * CHUNK, CHUNK)
        return pltpu.make_async_copy(tiles_hbm.at[part], tiles.at[part], tile_sem.at[k])

    def send(src, dst, send_sem, recv_sem, device):
        return pltpu.make_async_remote_copy(
            src_ref=src, dst_ref=dst, send_sem=send_sem, recv_sem=recv_sem,
            device_id=device, device_id_type=pl.DeviceIdType.MESH,
        )

    chunks = slots // CHUNK
    local = [
        pltpu.make_async_copy(cols_hbm, cols_v, local_sem.at[0]),
        pltpu.make_async_copy(rows_hbm, rows_v, local_sem.at[1]),
        pltpu.make_async_copy(weight_hbm, weight, local_sem.at[2]),
        pltpu.make_async_copy(feat_hbm, feats.at[row], local_sem.at[3]),
        pltpu.make_async_copy(count_hbm, count_s, local_sem.at[5]),
    ]
    for k in range(FIRST):
        tile_copy(k).start()
    for copy in local:
        copy.start()
    barrier = pltpu.get_barrier_semaphore()
    owners = [chip_peer(dy, dz) for dy, dz in ORDER[:-1]]
    y_next, y_prev, z_other = chip_peer(1, 0), chip_peer(3, 0), chip_peer(0, 1)
    partners = row_peers + [sibling, y_next, y_prev, z_other]
    for device in partners:
        pl.semaphore_signal(barrier, inc=1, device_id=device, device_id_type=pl.DeviceIdType.MESH)
    for k in range(FIRST, AHEAD):
        tile_copy(k).start()
    pl.semaphore_wait(barrier, len(partners))
    feat_copies = [
        send(feat_hbm, feats.at[row], feat_send.at[i], feat_recv.at[i], device)
        for i, device in enumerate(row_peers)
    ]
    for copy in feat_copies:
        copy.start()
    for k in range(AHEAD, chunks):
        tile_copy(k).start()

    def tell(sem, device):
        pl.semaphore_signal(sem, inc=1, device_id=device, device_id_type=pl.DeviceIdType.MESH)

    tell(y_two, y_prev)
    tell(z_one, z_other)

    tiles[slots] = jnp.zeros((SIDE, SIDE), BF16)
    scaled[:, SIDE:] = jnp.ones((col_tiles * SIDE, SIDE), BF16)
    sublane = lax.broadcasted_iota(I32, (8, SIDE), 0)

    def slot_sums(k, carry):
        tile_copy(k).wait()
        for g in range(CHUNK // 8):
            first = k * CHUNK + g * 8
            sums = None
            for s in range(8):
                tile = tiles[first + s].astype(F32)
                part = jnp.sum(tile.reshape(SIDE // 8, 8, SIDE), axis=0)
                part = jnp.broadcast_to(jnp.sum(part, axis=0, keepdims=True), (8, SIDE))
                sums = part if s == 0 else jnp.where(sublane == s, part, sums)
            csum[pl.ds(pl.multiple_of(first, 8), 8), :] = sums
        return carry

    def column_sums(first, end):
        size = end - first
        kind = lax.broadcasted_iota(I32, (col_tiles, size), 0)
        at = lax.broadcasted_iota(I32, (col_tiles, size), 1) + first
        pick = jnp.where((kind == cols_v[:, first:end]) & (at < count), 1.0, 0.0).astype(BF16)
        live = lax.broadcasted_iota(I32, (size, SIDE), 0) + first < count
        rest = jnp.where(live, csum[first:end], 0.0)
        total = jnp.zeros((col_tiles, SIDE), F32)
        for _ in range(3):
            piece = rest.astype(BF16)
            total = total + jnp.dot(pick, piece, preferred_element_type=F32)
            rest = rest - piece.astype(F32)
        return total

    late = (slots - 1) // SIDE * SIDE
    lax.fori_loop(0, 12, slot_sums, 0)

    for copy in local:
        copy.wait()
    count = count_s[0, 0]
    lane = lax.broadcasted_iota(I32, (1, slots), 1)
    place = jnp.where(lane < count, rows_v[...] * 32 + cols_v[...], -1)
    padded = jnp.concatenate([place, jnp.full((1, 7 * SIDE - slots), -1, I32)], axis=1)
    stacked = jnp.concatenate(
        [padded[:, g * SIDE:(g + 1) * SIDE] for g in range(7)] + [jnp.full((SIDE - 7, SIDE), -1, I32)], axis=0
    )
    turned = stacked.T
    places = [jnp.broadcast_to(turned[:, g:g + 1], (SIDE, SIDE)) for g in range(7)]
    slot_id = lax.broadcasted_iota(I32, (SIDE, SIDE), 0)
    lane_id = lax.broadcasted_iota(I32, (SIDE, SIDE), 1)
    slot_v[...] = jnp.full(slot_v.shape, slots, I32)

    def find(b, carry):
        best = jnp.full((SIDE, SIDE), slots, I32)
        for g in range(7):
            best = jnp.where(places[g] == lane_id + b * SIDE, slot_id + g * SIDE, best)
        slot_v[pl.ds(b, 1), :] = jnp.min(best, axis=0, keepdims=True)
        return carry

    lax.fori_loop(0, row_tiles * 32 // SIDE, find, 0)
    to_scalar = pltpu.make_async_copy(slot_v, slot_s, local_sem.at[4])
    to_scalar.start()


    lax.fori_loop(12, late // CHUNK, slot_sums, 0)
    own = column_sums(0, late)
    lax.fori_loop(late // CHUNK, chunks, slot_sums, 0)
    own = own + column_sums(late, slots)

    pl.semaphore_wait(y_two, 1)
    tell(z_two, z_other)

    colx[row] = own
    colx_copies = [
        send(colx.at[row], colx.at[row], colx_send.at[i], colx_recv.at[i], device)
        for i, device in enumerate(row_peers)
    ]
    for copy in colx_copies:
        copy.start()
    for copy in feat_copies:
        copy.wait_recv()

    def project(j, carry):
        projected[pl.ds(pl.multiple_of(j * group, group), group), :] = jnp.dot(
            feats[j], weight[...], preferred_element_type=F32
        )
        return carry

    lax.fori_loop(0, n_row, project, 0)
    to_scalar.wait()
    for copy in colx_copies:
        copy.wait_recv()
    degree = colx[0]
    for j in range(1, n_row):
        degree = degree + colx[j]
    factor = lax.rsqrt(1.0 + degree)
    factor = jnp.concatenate([factor, jnp.ones((SIDE - col_tiles, SIDE), F32)], axis=0).T
    for c in range(col_tiles):
        block = projected[c * SIDE:(c + 1) * SIDE, :] * factor[:, c:c + 1]
        scaled[c * SIDE:(c + 1) * SIDE, :SIDE] = block.astype(BF16)

    pl.semaphore_wait(z_one, 1)
    pl.semaphore_wait(z_two, 1)

    eye = jnp.where(slot_id == lane_id, 1.0, 0.0)

    def sib_copy(k):
        return send(full.at[k, 1 - core], sib.at[k], sib_send.at[k], sib_recv.at[k], sibling)

    def step_peer(k):
        return chip_peer(table(k, [d[0] for d in ORDER]), table(k, [d[1] for d in ORDER]))

    def owner_copy(k, device):
        return send(full.at[k, core], land.at[k], own_send.at[k], own_recv.at[k], device)

    def pair_sum(k):
        sib_copy(k).wait_recv()
        return full[k, core].astype(F32) + sib[k].astype(F32)

    def pass_on(k):
        total = pair_sum(k)
        full[k, core, pl.ds(0, group), :] = total[:group].astype(BF16)
        full[k, core, pl.ds(group, EXTRA), :] = split_sums(join_sums(total[group:]))
        owner_copy(k, step_peer(k)).start()

    def product(k, carry):
        first = (step_peer(k)[1] // 2) * step_tiles
        wide = []
        for a in range(step_tiles):
            at_row = first + a
            wide.append(jnp.concatenate(
                [tiles[slot_s[at_row // 4, (at_row % 4) * 32 + c]] for c in range(col_tiles)], axis=1
            ))
        result = jnp.dot(jnp.concatenate(wide, axis=0), scaled[...], preferred_element_type=F32)
        for h in range(2):
            part = result[h * group:(h + 1) * group]
            full[k, h, pl.ds(0, group), :] = part[:, :SIDE].astype(BF16)
            sums = [
                jnp.sum(part[i * SIDE:(i + 1) * SIDE, SIDE:] * eye, axis=0, keepdims=True)
                for i in range(owner_tiles)
            ]
            sums.append(jnp.zeros((8 - owner_tiles, SIDE), F32))
            full[k, h, pl.ds(group, EXTRA), :] = split_sums(jnp.concatenate(sums, axis=0))
        sib_copy(k).start()

        @pl.when(k > 0)
        def _():
            pass_on(k - 1)

        return carry

    lax.fori_loop(0, 8, product, 0)

    last = len(ORDER) - 1
    total = pair_sum(last)
    for k in range(last):
        owner_copy(k, owners[k]).wait_recv()
        total = total + land[k].astype(F32)
    norm = lax.rsqrt(1.0 + join_sums(total[group:]))
    norm = jnp.concatenate([norm, jnp.ones((SIDE - 8, SIDE), F32)], axis=0).T
    for i in range(owner_tiles):
        out_ref[i * SIDE:(i + 1) * SIDE, :] = (total[i * SIDE:(i + 1) * SIDE] * norm[:, i:i + 1]).astype(BF16)

    for copy in feat_copies + colx_copies:
        copy.wait_send()
    for k in range(len(ORDER)):
        sib_copy(k).wait_send()
    for k in range(last):
        owner_copy(k, owners[k]).wait_send()


def body(features, weight, tiles, tile_rows, tile_cols, tile_count):
    n_row, n_col = lax.axis_size("row"), lax.axis_size("col")
    group, width = features.shape
    hidden = weight.shape[1]
    slots, side = tiles.shape[2], tiles.shape[3]
    row_tiles = n_col * group // side
    col_tiles = n_row * group // side
    block = group + EXTRA
    dma = pltpu.SemaphoreType.DMA

    def run(*refs):
        kernel(n_row, n_col, slots, row_tiles, col_tiles, *refs)

    anywhere = pl.BlockSpec(memory_space=pl.ANY)
    return pl.pallas_call(
        run,
        out_shape=pltpu.VMEM((group, hidden), BF16),
        in_specs=[anywhere] * 5 + [pl.BlockSpec(memory_space=pltpu.HBM)],
        out_specs=pl.BlockSpec(memory_space=pltpu.VMEM),
        scratch_shapes=[
            pltpu.VMEM((slots + 1, side, side), BF16),
            pltpu.VMEM((slots, side), F32),
            pltpu.SMEM((1, 1), I32),
            pltpu.VMEM((n_row, group, width), BF16),
            pltpu.VMEM((width, hidden), BF16),
            pltpu.VMEM((col_tiles * side, hidden), F32),
            pltpu.VMEM((col_tiles * side, 2 * hidden), BF16),
            pltpu.VMEM((1, slots), I32),
            pltpu.VMEM((1, slots), I32),
            pltpu.VMEM((16, side), I32),
            pltpu.SMEM((16, side), I32),
            pltpu.VMEM((n_row, col_tiles, side), F32),
            pltpu.VMEM((8, 2, block, hidden), BF16),
            pltpu.VMEM((8, block, hidden), BF16),
            pltpu.VMEM((7, block, hidden), BF16),
            dma((slots // CHUNK,)),
            dma((6,)),
            dma((n_row - 1,)),
            dma((n_row - 1,)),
            dma((n_row - 1,)),
            dma((n_row - 1,)),
            dma((8,)),
            dma((8,)),
            dma((7,)),
            dma((7,)),
            pltpu.SemaphoreType.REGULAR,
            pltpu.SemaphoreType.REGULAR,
            pltpu.SemaphoreType.REGULAR,
        ],
        compiler_params=pltpu.CompilerParams(
            collective_id=0, has_side_effects=True, vmem_limit_bytes=56 * 2**20
        ),
    )(
        features, weight, tiles.reshape(slots, side, side),
        tile_rows.reshape(1, slots), tile_cols.reshape(1, slots), tile_count.reshape(1, 1),
    )


def solution(mesh):
    in_specs = (
        P(("col", "row"), None),
        P(),
        P("row", "col", None, None, None),
        P("row", "col", None),
        P("row", "col", None),
        P("row", "col"),
    )
    out_specs = P(("row", "col"), None)
    return jax.shard_map(body, mesh=mesh, in_specs=in_specs, out_specs=out_specs, check_vma=False)
```

time: 49.1 us -> 38.8 us (0.79)
  the two profiles are of different devices: /device:TPU:0 before, /device:TPU:1 now
where the time goes in v1:
time: 38.8 us; the launch traced here: 38.7 us
  Pallas kernels  37.4 us (96%)
  between operations  0.66 us (2%)
  local copies, waits for them, and re-layouts  0.64 us (2%)
    pallas_call x1, Pallas kernels, body(): pl.pallas_call(run, out_shape=pltpu.VMEM((group, hidden), BF16), in_specs...  37.4 us

profile of v1, /device:TPU:1, one launch (start us, length us, event | category | flops | bytes accessed | tf_op | source)
XLA Modules:
  0.0 38.7 jit_solution(10346585140858720676)
XLA Ops:
  0.7 37.4 %shard_map.64 = bf16[384,128]{1,0:T(8,128)(2,1)S(1)} custom-call(bf16[384,128]{1,0:T(8,128)(2,1)} %refs_0_.1, bf16[128,128]{1,0:T(8,128)(2,1)} %refs_1_.1, bf16[864,128,128]{2,1,0:T(8,128)(2,1)} %bitcast.3, s32[1,864]{1,0:T(1,128)} %bitcast.4, s32[1,864]{1,0:T(1,128)} %bitcast.5, s32[1,1]{1,0:T(1,128)S(6)} %copy.9.refs_5_), custom_call_target="tpu_custom_call" | custom-call | tf_op jit(solution)/shard_map/pallas_call | solution.py:296
  38.1 0.6 %copy.8 = bf16[384,128]{1,0:T(8,128)(2,1)} copy(bf16[384,128]{1,0:T(8,128)(2,1)S(1)} %shard_map.64) | data formatting | bytes 196608

commit v2 on v1

--- a/solution.py
+++ b/solution.py
@@ -11,7 +11,7 @@
 EXTRA = 16
 FIRST = 3
 AHEAD = 10
-ORDER = ((2, 1), (1, 1), (3, 1), (2, 0), (0, 1), (1, 0), (3, 0), (0, 0))
+ORDER = ((2, 1), (0, 1), (2, 0), (1, 1), (3, 1), (1, 0), (3, 0), (0, 0))
 
 
 def table(step, values):

time: 38.8 us -> 38.1 us (0.982)
  Pallas kernels: 37.4 us -> 36.7 us
    pallas_call x1, Pallas kernels: 37.4 us -> 36.7 us  [body(): pl.pallas_call(run, out_shape=pltpu.VMEM((group, hidden), BF16), in_specs...]
where the time goes in v2:
time: 38.1 us; the launch traced here: 38 us
  Pallas kernels  36.7 us (96%)
  between operations  0.66 us (2%)
  local copies, waits for them, and re-layouts  0.64 us (2%)
    pallas_call x1, Pallas kernels, body(): pl.pallas_call(run, out_shape=pltpu.VMEM((group, hidden), BF16), in_specs...  36.7 us

profile of v2, /device:TPU:1, one launch (start us, length us, event | category | flops | bytes accessed | tf_op | source)
XLA Modules:
  0.0 38.0 jit_solution(13448263935833691462)
XLA Ops:
  0.7 36.7 %shard_map.64 = bf16[384,128]{1,0:T(8,128)(2,1)S(1)} custom-call(bf16[384,128]{1,0:T(8,128)(2,1)} %refs_0_.1, bf16[128,128]{1,0:T(8,128)(2,1)} %refs_1_.1, bf16[864,128,128]{2,1,0:T(8,128)(2,1)} %bitcast.3, s32[1,864]{1,0:T(1,128)} %bitcast.4, s32[1,864]{1,0:T(1,128)} %bitcast.5, s32[1,1]{1,0:T(1,128)S(6)} %copy.9.refs_5_), custom_call_target="tpu_custom_call" | custom-call | tf_op jit(solution)/shard_map/pallas_call | solution.py:296
  37.4 0.6 %copy.8 = bf16[384,128]{1,0:T(8,128)(2,1)} copy(bf16[384,128]{1,0:T(8,128)(2,1)S(1)} %shard_map.64) | data formatting | bytes 196608

commit v3 on v2

--- a/solution.py
+++ b/solution.py
@@ -262,10 +262,16 @@
     lax.fori_loop(0, 8, product, 0)
 
     last = len(ORDER) - 1
-    total = pair_sum(last)
-    for k in range(last):
-        owner_copy(k, owners[k]).wait_recv()
-        total = total + land[k].astype(F32)
+    sum_rows = pl.ds(0, group + EXTRA)
+    projected[sum_rows, :] = pair_sum(last)
+
+    def collect(k, carry):
+        owner_copy(k, step_peer(k)).wait_recv()
+        projected[sum_rows, :] += land[k].astype(F32)
+        return carry
+
+    lax.fori_loop(0, last, collect, 0)
+    total = projected[sum_rows, :]
     norm = lax.rsqrt(1.0 + join_sums(total[group:]))
     norm = jnp.concatenate([norm, jnp.ones((SIDE - 8, SIDE), F32)], axis=0).T
     for i in range(owner_tiles):

time: 38.1 us -> 38.2 us (level)
  no operation moved by 1% of the time
where the time goes in v3:
time: 38.2 us; the launch traced here: 38.1 us
  Pallas kernels  36.8 us (96%)
  between operations  0.66 us (2%)
  local copies, waits for them, and re-layouts  0.64 us (2%)
    pallas_call x1, Pallas kernels, body(): pl.pallas_call(run, out_shape=pltpu.VMEM((group, hidden), BF16), in_specs...  36.8 us

profile of v3, /device:TPU:1, one launch (start us, length us, event | category | flops | bytes accessed | tf_op | source)
XLA Modules:
  0.0 38.1 jit_solution(3689159270807339496)
XLA Ops:
  0.7 36.8 %shard_map.64 = bf16[384,128]{1,0:T(8,128)(2,1)S(1)} custom-call(bf16[384,128]{1,0:T(8,128)(2,1)} %refs_0_.1, bf16[128,128]{1,0:T(8,128)(2,1)} %refs_1_.1, bf16[864,128,128]{2,1,0:T(8,128)(2,1)} %bitcast.3, s32[1,864]{1,0:T(1,128)} %bitcast.4, s32[1,864]{1,0:T(1,128)} %bitcast.5, s32[1,1]{1,0:T(1,128)S(6)} %copy.9.refs_5_), custom_call_target="tpu_custom_call" | custom-call | tf_op jit(solution)/shard_map/pallas_call | solution.py:302
  37.4 0.6 %copy.8 = bf16[384,128]{1,0:T(8,128)(2,1)} copy(bf16[384,128]{1,0:T(8,128)(2,1)S(1)} %shard_map.64) | data formatting | bytes 196608
